TPU v7x, 32 devices: a whole 2x2x4 slice. The times are simulated.
32 devices in a mesh: dp: 4 (over z), tensor: 8 (over y, x, core).
Axes of the slice: x: 2, y: 2, z: 4, core: 2. Of those that a mesh axis runs over, the one named last changes fastest.
Arguments:
- tokens: bfloat16 [512, 8192], P('dp'), may hold values from -6 to 6
- hidden_grad: bfloat16 [512, 14336], P('dp', 'tensor'), may hold values from -6 to 6
- gate_weight: bfloat16 [8192, 14336], P('dp', 'tensor'), may hold values from -0.0625 to 0.0625
- up_weight: bfloat16 [8192, 14336], P('dp', 'tensor'), may hold values from -0.0625 to 0.0625
- proj_in: bfloat16 [2, 8192, 64], P(None, 'tensor'), may hold values from -0.005859375 to 0.005859375
- proj_out: bfloat16 [2, 14336, 64], P(None, 'tensor'), may hold values from -0.046875 to 0.046875
Outputs:
- input_grad: bfloat16 [512, 8192], P('dp', 'tensor')
- features: float32 [4, 2, 64, 64], P('dp', None, 'tensor')
All inputs are finite; a program needn't handle non-finite values.
Results may differ from a plain program's by a relative error of at most 0.012.
Values may be sent and summed in bfloat16 or wider, within the bound.
A program may use at most 192 MiB of HBM per device.

v0:
```python
import jax
import jax.numpy as jnp
from jax import lax
from jax.sharding import PartitionSpec as P

SEQ_LEN = 128
F32 = jnp.float32
BF16 = jnp.bfloat16


def shards(n_dp, n_tensor, tokens, hidden_grad, gate_weight, up_weight, proj_in, proj_out):
    highest = lax.Precision.HIGHEST
    place = lax.axis_index("tensor")
    rows, width = tokens.shape
    rank = proj_in.shape[2]
    block = width // n_dp
    band = width // n_tensor
    halves = n_tensor // n_dp
    share = rows // n_tensor

    mine = lax.dynamic_slice_in_dim(tokens, place * share, share, 0)
    mine = mine.reshape(share, n_dp, block).transpose(1, 0, 2)
    mine = lax.all_to_all(mine, "dp", 0, 0)
    tok = lax.all_gather(mine, "tensor", axis=1, tiled=True).reshape(n_dp * rows, block)

    gate_part = jnp.dot(tok, gate_weight, preferred_element_type=F32).astype(BF16)
    up_part = jnp.dot(tok, up_weight, preferred_element_type=F32).astype(BF16)
    gate = lax.psum_scatter(gate_part, "dp", scatter_dimension=0, tiled=True).astype(F32)
    up = lax.psum_scatter(up_part, "dp", scatter_dimension=0, tiled=True).astype(F32)
    cotan = hidden_grad.astype(F32)
    sigm = jax.nn.sigmoid(gate)
    d_gate = (cotan * up * sigm * (1.0 + gate * (1.0 - sigm))).astype(BF16)
    d_up = (cotan * gate * sigm).astype(BF16)
    d_gate_all = lax.all_gather(d_gate, "dp", axis=0, tiled=True)
    d_up_all = lax.all_gather(d_up, "dp", axis=0, tiled=True)
    term = jnp.einsum("tf,df->td", d_gate_all, gate_weight, preferred_element_type=F32)
    term = (term + jnp.einsum("tf,df->td", d_up_all, up_weight, preferred_element_type=F32)).astype(BF16)
    term = term.reshape(n_dp, rows, halves, band).transpose(0, 2, 1, 3).reshape(n_tensor * rows, band)
    piece = lax.psum_scatter(term, "tensor", scatter_dimension=0, tiled=True)
    pairs = []
    for i in range(n_dp):
        for m in range(n_tensor):
            p, h = divmod(m, halves)
            pairs.append((i * n_tensor + m, p * n_tensor + i * halves + h))
    input_grad = lax.ppermute(piece, ("dp", "tensor"), pairs)

    local_cols = lax.dynamic_slice_in_dim(tokens, place * band, band, 1)
    in_partial = jnp.einsum("td,kda->tka", local_cols, proj_in, preferred_element_type=F32)
    projected_in = lax.psum(in_partial, "tensor")
    grad_partial = jnp.stack(
        [
            jnp.dot(d_gate, proj_out[0], preferred_element_type=F32),
            jnp.dot(d_up, proj_out[1], preferred_element_type=F32),
        ],
        axis=1,
    )
    seqs = rows // SEQ_LEN
    seq_in = projected_in.reshape(seqs, SEQ_LEN, 2, rank)
    seq_grad = grad_partial.reshape(seqs, SEQ_LEN, 2, rank)
    terms = jnp.einsum("slka,slkb->skab", seq_in, seq_grad, precision=highest)
    features = lax.psum_scatter(terms, "tensor", scatter_dimension=2, tiled=True)
    return (input_grad, features)


def solution(mesh):
    placed = (
        P("dp", None),
        P("dp", "tensor"),
        P("dp", "tensor"),
        P("dp", "tensor"),
        P(None, "tensor", None),
        P(None, "tensor", None),
    )

    def body(*args):
        return shards(mesh.shape["dp"], mesh.shape["tensor"], *args)

    return jax.shard_map(
        body,
        mesh=mesh,
        in_specs=placed,
        out_specs=(P("dp", "tensor"), P("dp", None, "tensor", None)),
        check_vma=False,
    )
```

profile of v0, /device:TPU:7, one launch (start us, length us, event | category | flops | bytes accessed | tf_op | source)
XLA Modules:
  0.0 384.9 jit_solution(376472265233115346)
XLA Ops:
  7.2 0.0 copy-start
  7.2 0.0 all-gather.4.cloned.1.call-start
  7.2 1.5 copy-done
  8.8 0.2 reshape.23
  9.0 0.2 copy.12
  9.1 11.3 %all_to_all.5 = bf16[4,16,2048]{2,1,0:T(8,128)(2,1)S(1)} all-to-all(bf16[4,16,2048]{2,1,0:T(8,128)(2,1)S(1)} %copy.12), channel_id=1, replica_groups=mesh['dp'=4,'tensor'=8] {'dp'}, dimensions={0} | all-to-all | bytes 524288 | tf_op jit(solution)/shard_map/all_to_all | solution.py:23
  20.4 0.9 copy.13
  21.3 0.0 all-gather.4.cloned.1.call-update
  21.3 0.0 reduce-scatter.5.cloned.1.call-start
  21.4 28.8 %all-gather.4.cloned.1.call-done = bf16[4,128,2048]{2,0,1:T(4,128)(2,1)} async-done(((bf16[4,16,2048]{2,0,1:T(4,128)(2,1)}), bf16[4,128,2048]{2,0,1:T(4,128)(2,1)}) %all-gather.4.cloned.1.call-update) | async-done | bytes 2097168 | tf_op jit(solution)/shard_map/all_gather | solution.py:24
  50.2 2.7 copy.14
  52.9 0.0 copy-start.3
  53.0 1.3 copy-done.3
  54.3 8.2 %convolution_convert_fusion.1 = bf16[512,1792]{1,0:T(8,128)(2,1)} fusion(bf16[512,2048]{1,0:T(8,128)(2,1)S(1)} %bitcast.34, bf16[2048,1792]{1,0:T(8,128)(2,1)} %param.9), kind=kOutput, calls=%fused_computation.2 | convolution fusion | flops 3759013888 | bytes 11272192 | tf_op jit(solution)/shard_map/dot_general | solution.py:27
  62.5 0.0 reduce-scatter.5.cloned.1.call-update
  62.5 0.0 reduce-scatter.7.cloned.1.call-start
  62.5 9.0 %convolution_convert_fusion = bf16[512,1792]{1,0:T(8,128)(2,1)} fusion(bf16[512,2048]{1,0:T(8,128)(2,1)} %bitcast.35, bf16[2048,1792]{1,0:T(8,128)(2,1)} %param.8), kind=kOutput, calls=%fused_computation.1 | convolution fusion | flops 3759013888 | bytes 11272192 | tf_op jit(solution)/shard_map/dot_general | solution.py:26
  71.5 0.0 copy-start.5
  71.5 0.0 reduce-scatter.7.cloned.1.call-update
  71.5 0.0 all-gather.6.cloned.1.call-start
  71.6 30.8 %reduce-scatter.5.cloned.1.call-done = bf16[128,1792]{1,0:T(8,128)(2,1)} async-done(((bf16[512,1792]{1,0:T(8,128)(2,1)}), bf16[128,1792]{1,0:T(8,128)(2,1)}) %reduce-scatter.5.cloned.1.call-update) | async-done | bytes 458768 | tf_op jit(solution)/shard_map/reduce_scatter | solution.py:29
  102.4 40.9 %reduce-scatter.7.cloned.1.call-done = bf16[128,1792]{1,0:T(8,128)(2,1)} async-done(((bf16[512,1792]{1,0:T(8,128)(2,1)}), bf16[128,1792]{1,0:T(8,128)(2,1)}) %reduce-scatter.7.cloned.1.call-update) | async-done | bytes 458768 | tf_op jit(solution)/shard_map/reduce_scatter | solution.py:28
  143.3 0.0 copy-done.5
  143.3 2.6 fusion.8
  145.9 0.0 all-gather.6.cloned.1.call-update
  145.9 0.0 all-gather.8.cloned.1.call-start
  146.0 0.5 all-gather.8.cloned.1.call-update
  146.5 0.2 reduce-scatter.9.cloned.1.call-start
  146.7 40.0 %all-gather.6.cloned.1.call-done = bf16[512,1792]{1,0:T(8,128)(2,1)} async-done(((bf16[128,1792]{1,0:T(8,128)(2,1)}), bf16[512,1792]{1,0:T(8,128)(2,1)}) %all-gather.6.cloned.1.call-update) | async-done | bytes 1835024 | tf_op jit(solution)/shard_map/all_gather | solution.py:34
  186.8 9.6 %fusion.20 = f32[512,2048]{1,0:T(8,128)} fusion(bf16[512,1792]{1,0:T(8,128)(2,1)} %all-gather.6.cloned.1.call-done, bf16[2048,1792]{1,0:T(8,128)(2,1)} %param.8), kind=kOutput, calls=%fused_computation.31 | convolution fusion | flops 3758096384 | bytes 13369344 | tf_op jit(solution)/shard_map/tf,df->td/dot_general | solution.py:36
  196.4 32.1 %all-gather.8.cloned.1.call-done = bf16[512,1792]{1,0:T(8,128)(2,1)} async-done(((bf16[128,1792]{1,0:T(8,128)(2,1)}), bf16[512,1792]{1,0:T(8,128)(2,1)}) %all-gather.8.cloned.1.call-update) | async-done | bytes 1835024 | tf_op jit(solution)/shard_map/all_gather | solution.py:35
  228.5 10.1 %add_convert_fusion = bf16[512,2048]{1,0:T(8,128)(2,1)} fusion(f32[512,2048]{1,0:T(8,128)} %fusion.20, bf16[512,1792]{1,0:T(8,128)(2,1)} %all-gather.8.cloned.1.call-done, bf16[2048,1792]{1,0:T(8,128)(2,1)} %param.9), kind=kOutput, calls=%fused_computation | convolution fusion | flops 3760193536 | bytes 15466496 | tf_op jit(solution)/shard_map/tf,df->td/dot_general | solution.py:37
  238.6 4.5 %reshape.25 = bf16[4,128,2,1024]{3,2,1,0:T(2,128)(2,1)} reshape(bf16[512,2048]{1,0:T(8,128)(2,1)} %add_convert_fusion) | data formatting | bytes 4194304 | tf_op jit(solution)/shard_map/reshape | solution.py:38
  243.1 3.6 copy.15
  246.7 0.0 copy-start.2
  246.7 0.0 copy-start.4
  246.7 0.0 copy-start.1
  246.7 0.0 reduce-scatter.9.cloned.1.call-update
  246.7 0.0 all-reduce.2.cloned.1.call-start
  246.8 1.9 fusion.9
  248.7 0.0 all-reduce.2.cloned.1.call-update
  248.7 0.0 reduce-scatter.11.cloned.1.call-start
  248.8 0.0 copy-done.2
  248.8 0.0 copy-done.4
  248.8 0.3 convolution_bitcast_fusion.1
  249.1 37.0 %reduce-scatter.9.cloned.1.call-done = bf16[128,1024]{1,0:T(8,128)(2,1)} async-done(((bf16[1024,1024]{1,0:T(8,128)(2,1)}), bf16[128,1024]{1,0:T(8,128)(2,1)}) %reduce-scatter.9.cloned.1.call-update) | async-done | bytes 262160 | tf_op jit(solution)/shard_map/reduce_scatter | solution.py:39
  286.1 5.8 %collective-permute-start = (bf16[128,1024]{1,0:T(8,128)(2,1)}, bf16[128,1024]{1,0:T(8,128)(2,1)S(1)}, u32[]{:S(2)}, u32[]{:S(2)}) collective-permute-start(bf16[128,1024]{1,0:T(8,128)(2,1)} %reduce-scatter.9.cloned.1.call-done), channel_id=1, source_target_pairs={{0,0},{1,1},{2,8},{3,9},{4,16},{5,17},{6,24},{7,25},{8,2},{9,3},{1... | collective-permute-start | bytes 786440 | tf_op jit(solution)/shard_map/ppermute | solution.py:45
  291.9 0.0 copy-done.1
  291.9 0.3 convolution_bitcast_fusion.2
  292.2 49.9 %all-reduce.2.cloned.1.call-done = f32[128,2,64]{0,2,1:T(8,128)} async-done(((f32[128,2,64]{0,2,1:T(8,128)}), f32[128,2,64]{0,2,1:T(8,128)}) %all-reduce.2.cloned.1.call-update) | async-done | bytes 65552 | tf_op jit(solution)/shard_map/psum | solution.py:49
  342.1 1.7 convolution_bitcast_fusion
  343.8 0.0 reduce-scatter.11.cloned.1.call-update
  343.8 0.0 collective-permute-done
  343.8 33.6 %reduce-scatter.11.cloned.1.call-done = f32[1,2,8,64]{3,2,1,0:T(8,128)} async-done(((f32[1,2,64,64]{3,2,1,0:T(8,128)}), f32[1,2,8,64]{3,2,1,0:T(8,128)}) %reduce-scatter.11.cloned.1.call-update) | async-done | bytes 4112 | tf_op jit(solution)/shard_map/reduce_scatter | solution.py:61
  377.4 0.7 copy.18
  (1 shorter events, 0.0 us)
Async XLA Ops:
  7.2 1.6 copy-start
  7.2 43.0 %all-gather.4.cloned.1.call-start = ((), (), s32[]{:S(2)}) async-start(), calls=%async_computation.5 | async-start | bytes 2359296 | tf_op jit(solution)/shard_map/all_gather | solution.py:24
  21.3 81.1 %reduce-scatter.5.cloned.1.call-start = ((), (), s32[]{:S(2)}) async-start(), calls=%async_computation.6 | async-start | bytes 2293760 | tf_op jit(solution)/shard_map/reduce_scatter | solution.py:29
  52.9 1.3 copy-start.3
  62.5 80.8 %reduce-scatter.7.cloned.1.call-start = ((), (), s32[]{:S(2)}) async-start(), calls=%async_computation.7 | async-start | bytes 2293760 | tf_op jit(solution)/shard_map/reduce_scatter | solution.py:28
  71.5 71.8 %copy-start.5 = (bf16[128,1792]{1,0:T(8,128)(2,1)S(1)}, bf16[128,1792]{1,0:T(8,128)(2,1)}, u32[]{:S(2)}) copy-start(bf16[128,1792]{1,0:T(8,128)(2,1)} %param.7) | copy-start | bytes 1376260
  71.5 115.3 %all-gather.6.cloned.1.call-start = ((), (), s32[]{:S(2)}) async-start(), calls=%async_computation.8 | async-start | bytes 2293760 | tf_op jit(solution)/shard_map/all_gather | solution.py:34
  145.9 82.6 %all-gather.8.cloned.1.call-start = ((), (), s32[]{:S(2)}) async-start(), calls=%async_computation.9 | async-start | bytes 2293760 | tf_op jit(solution)/shard_map/all_gather | solution.py:35
  146.5 139.5 %reduce-scatter.9.cloned.1.call-start = ((), (), s32[]{:S(2)}) async-start(), calls=%async_computation.10 | async-start | bytes 2359296 | tf_op jit(solution)/shard_map/reduce_scatter | solution.py:39
  246.7 2.1 copy-start.2
  246.7 2.1 copy-start.4
  246.7 45.2 %copy-start.1 = (bf16[128,1792]{1,0:T(8,128)(2,1)S(1)}, bf16[128,1792]{1,0:T(8,128)(2,1)}, u32[]{:S(2)}) copy-start(bf16[128,1792]{1,0:T(8,128)(2,1)} %get-tuple-element.3) | copy-start | bytes 1376260
  246.7 95.4 %all-reduce.2.cloned.1.call-start = ((), (), s32[]{:S(2)}) async-start(), calls=%async_computation.11 | async-start | bytes 131072 | tf_op jit(solution)/shard_map/psum | solution.py:49
  248.7 128.7 %reduce-scatter.11.cloned.1.call-start = ((), (), s32[]{:S(2)}) async-start(), calls=%async_computation.12 | async-start | bytes 73728 | tf_op jit(solution)/shard_map/reduce_scatter | solution.py:61
  286.1 57.8 %collective-permute-start = (bf16[128,1024]{1,0:T(8,128)(2,1)}, bf16[128,1024]{1,0:T(8,128)(2,1)S(1)}, u32[]{:S(2)}, u32[]{:S(2)}) collective-permute-start(bf16[128,1024]{1,0:T(8,128)(2,1)} %reduce-scatter.9.cloned.1.call-done), channel_id=1, source_target_pairs={{0,0},{1,1},{2,8},{3,9},{4,16},{5,17},{6,24},{7,25},{8,2},{9,3},{1... | collective-permute-start | bytes 786440 | tf_op jit(solution)/shard_map/ppermute | solution.py:45
Sparse Core Ops, SparseCore 0:
  21.5 28.7 all-gather.3
  62.6 39.7 reduce-scatter.4
  104.7 38.5 reduce-scatter.6
  146.1 40.6 all-gather.5
  188.2 40.2 all-gather.7
  246.9 39.1 reduce-scatter.8
  290.0 52.0 all-reduce.1
  345.7 31.6 reduce-scatter.10
where the time goes:
time: 388 us; the launch traced here: 385 us
  waiting for transfers between devices  294 us (76%)
  matrix products  41 us (11%)
  local copies, waits for them, and re-layouts  15.7 us (4%)
  between operations  14.2 us (4%)
  blocking collectives  11.3 us (3%)
  starting transfers between devices  6.35 us (2%)
    psum x1, waiting for transfers between devices, shards(): projected_in = lax.psum(in_partial, 'tensor')  49.9 us
    reduce_scatter x1, waiting for transfers between devices, shards(): lax.psum_scatter(gate_part, 'dp', scatter_dimension=0, tiled=True)  40.9 us
    all_gather x1, waiting for transfers between devices, shards(): d_gate_all = lax.all_gather(d_gate, 'dp', axis=0, tiled=True)  40 us
    reduce_scatter x1, waiting for transfers between devices, shards(): piece = lax.psum_scatter(term, 'tensor', scatter_dimension=0, tiled=True)  37 us
    reduce_scatter x1, waiting for transfers between devices, shards(): lax.psum_scatter(terms, 'tensor', scatter_dimension=2, tiled=True)  33.6 us
    all_gather x1, waiting for transfers between devices, shards(): d_up_all = lax.all_gather(d_up, 'dp', axis=0, tiled=True)  32.1 us
    reduce_scatter x1, waiting for transfers between devices, shards(): lax.psum_scatter(up_part, 'dp', scatter_dimension=0, tiled=True).astype(F32)  30.8 us
    all_gather x1, waiting for transfers between devices, shards(): lax.all_gather(mine, 'tensor', axis=1, tiled=True)  28.8 us
  transfers between devices with their start and end apart: 9, of which 8 were waited for; matrix products, arithmetic and copies ran while one was open for 6% of the time, Pallas kernels for 0%

commit v1 on v0

--- a/solution.py
+++ b/solution.py
@@ -1,6 +1,10 @@
+import functools
+
 import jax
 import jax.numpy as jnp
 from jax import lax
+from jax.experimental import pallas as pl
+from jax.experimental.pallas import tpu as pltpu
 from jax.sharding import PartitionSpec as P
 
 SEQ_LEN = 128
@@ -62,6 +66,396 @@
     return (input_grad, features)
 
 
+ROUND = 16
+TILE = 256
+NDP = 4
+NT = 8
+
+
+def fused(
+    tokens, hidden, gate_hbm, up_hbm, proj_in, proj_out, grad_out, feat_out,
+    wg, wu, tok, acc, part, recv, dval, term, landed, fin, fin_land,
+    pin_send, pin_recv, pin_all, feat_send, feat_recv,
+    w_sem, a1_send, a1_recv, a2_send, a2_recv, red_send, red_recv,
+    root_send, fwd_send, bc_recv, rs_send, rs_recv, fin_send, fin_recv,
+    ps_send, ps_recv, pa_send, pa_recv, ft_send, ft_recv,
+):
+    z, t = lax.axis_index("dp"), lax.axis_index("tensor")
+    rows, width = tokens.shape
+    block, hid = wg.shape
+    band = width // NT
+    rank = proj_in.shape[2]
+    share = rows // NT
+    rounds = rows // ROUND
+    brows = 2 * ROUND
+    mid = jnp.logical_and(z > 0, z < NDP - 1)
+    edge = jnp.logical_or(z == 0, z == NDP - 1)
+    low = z // 2
+    o0 = 3 - 3 * low
+    o2 = z + 1 - 2 * low
+    o1 = 6 - z - o0 - o2
+    ways = (1 - 2 * low, 1 - 2 * (z % 2), 1 - 2 * low)
+    dests = (o0, o1, o2)
+    is1 = (z % 2) * (1 - low)
+    slots = (o0, o1 + (4 - o1) * is1, o2 + (4 - o2) * low)
+    pz, pt = t // 2, 2 * z + t % 2
+    away = pz != z
+
+    def remote(src, dst, ssem, rsem, dz, dt):
+        return pltpu.make_async_remote_copy(
+            src_ref=src, dst_ref=dst, send_sem=ssem, recv_sem=rsem,
+            device_id=(dz, dt), device_id_type=pl.DeviceIdType.MESH,
+        )
+
+    def drain(ref, sem):
+        pltpu.make_async_copy(ref, ref, sem).wait()
+
+    def peers(fn):
+        def step(d, c):
+            fn(lax.rem(t + d, NT))
+            return c
+
+        lax.fori_loop(1, NT, step, 0)
+
+    cg = pltpu.make_async_copy(gate_hbm, wg, w_sem.at[0])
+    cu = pltpu.make_async_copy(up_hbm, wu, w_sem.at[1])
+    cg.start()
+    cu.start()
+
+    barrier = pltpu.get_barrier_semaphore()
+
+    def hello(dz, dt):
+        pl.semaphore_signal(barrier, inc=1, device_id=(dz, dt), device_id_type=pl.DeviceIdType.MESH)
+
+    peers(lambda q: hello(z, q))
+    for d in range(1, NDP):
+        hello(lax.rem(z + d, NDP), t)
+
+    @pl.when(away)
+    def _():
+        hello(pz, pt)
+        pl.semaphore_wait(barrier, NT + NDP - 1)
+
+    @pl.when(jnp.logical_not(away))
+    def _():
+        pl.semaphore_wait(barrier, NT + NDP - 2)
+
+    my_rows = pl.ds(pl.multiple_of(t * share, share), share)
+    for d in range(1, NDP):
+        i = lax.rem(z + d, NDP)
+        remote(
+            tokens.at[my_rows, pl.ds(pl.multiple_of(i * block, block), block)],
+            tok.at[z, my_rows, :], a1_send.at[d - 1], a1_recv.at[z], i, t,
+        ).start()
+
+    cols = tokens[:, pl.ds(pl.multiple_of(t * band, band), band)]
+    pin = jnp.concatenate(
+        [jnp.dot(cols, proj_in[k], preferred_element_type=F32) for k in range(2)], axis=1
+    ).T
+    for q in range(NT):
+        for k in range(2):
+            lo = k * rank + q * (rank // NT)
+            pin_send[q, k] = pin[lo : lo + rank // NT]
+    peers(lambda q: remote(pin_send.at[q], pin_recv.at[t], ps_send, ps_recv, z, q).start())
+
+    for p in dests:
+        drain(tok.at[p, my_rows, :], a1_recv.at[p])
+        peers(
+            lambda q: remote(
+                tok.at[p, my_rows, :], tok.at[p, my_rows, :], a2_send.at[p], a2_recv.at[p], z, q
+            ).start()
+        )
+    cg.wait()
+    cu.wait()
+
+    def forward(p, x):
+        def tile(c, carry):
+            at = pl.ds(pl.multiple_of(c * TILE, TILE), TILE)
+            acc[p, 0, :, at] = jnp.dot(x(), wg[:, at], preferred_element_type=F32)
+            acc[p, 1, :, at] = jnp.dot(x(), wu[:, at], preferred_element_type=F32)
+            return carry
+
+        lax.fori_loop(0, hid // TILE, tile, 0)
+
+    def at_round(r):
+        return pl.ds(pl.multiple_of(r * ROUND, ROUND), ROUND)
+
+    def reduce(k, r):
+        p, sl = dests[k], at_round(r)
+
+        @pl.when(mid)
+        def _():
+            drain(recv.at[p, :, sl, :], red_recv.at[p, r])
+            part[k, :, sl, :] = (acc[p, :, sl, :] + recv[p, :, sl, :].astype(F32)).astype(BF16)
+
+        @pl.when(edge)
+        def _():
+            part[k, :, sl, :] = acc[p, :, sl, :].astype(BF16)
+
+        remote(
+            part.at[k, :, sl, :], recv.at[slots[k], :, sl, :],
+            red_send.at[k, r], red_recv.at[slots[k], r], z + ways[k], t,
+        ).start()
+
+    def bcast(p, r, ssem, dz):
+        sl = at_round(r)
+        remote(dval.at[p, :, sl, :], dval.at[p, :, sl, :], ssem, bc_recv.at[p, r], dz, t).start()
+
+    def root(r):
+        sl = at_round(r)
+
+        @pl.when(z > 0)
+        def _():
+            drain(recv.at[z, :, sl, :], red_recv.at[z, r])
+            acc[z, :, sl, :] = acc[z, :, sl, :] + recv[z, :, sl, :].astype(F32)
+
+        @pl.when(z < NDP - 1)
+        def _():
+            drain(recv.at[4, :, sl, :], red_recv.at[4, r])
+            acc[z, :, sl, :] = acc[z, :, sl, :] + recv[4, :, sl, :].astype(F32)
+
+        gate, up = acc[z, 0, sl, :], acc[z, 1, sl, :]
+        cotan = hidden[sl, :].astype(F32)
+        sigm = jax.nn.sigmoid(gate)
+        dval[z, 0, sl, :] = (cotan * up * sigm * (1.0 + gate * (1.0 - sigm))).astype(BF16)
+        dval[z, 1, sl, :] = (cotan * gate * sigm).astype(BF16)
+
+        @pl.when(z < NDP - 1)
+        def _():
+            bcast(z, r, root_send.at[0, r], z + 1)
+
+        @pl.when(z > 0)
+        def _():
+            bcast(z, r, root_send.at[1, r], z - 1)
+
+    def onward(r):
+        for k in (2, 1, 0):
+            p = dests[k]
+            drain(dval.at[p, :, at_round(r), :], bc_recv.at[p, r])
+
+            @pl.when(mid)
+            def _():
+                bcast(p, r, fwd_send.at[k, r], z - ways[k])
+
+    def at_block(b):
+        return pl.ds(pl.multiple_of(b * brows, brows), brows)
+
+    def backward(b):
+        sl = at_block(b)
+        per = band // TILE
+
+        def tile(c, carry):
+            at = pl.ds(pl.multiple_of(c * TILE, TILE), TILE)
+            nt = (((1,), (1,)), ((), ()))
+            dg = jnp.concatenate([dval[p, 0, sl, :] for p in range(NDP)], axis=0)
+            du = jnp.concatenate([dval[p, 1, sl, :] for p in range(NDP)], axis=0)
+            out = lax.dot_general(dg, wg[at, :], nt, preferred_element_type=F32)
+            out = out + lax.dot_general(du, wu[at, :], nt, preferred_element_type=F32)
+            out = out.astype(BF16)
+            to = pl.ds(pl.multiple_of((c % per) * TILE, TILE), TILE)
+            for p in range(NDP):
+                term[2 * p + c // per, sl, to] = out[p * brows : (p + 1) * brows]
+            return carry
+
+        lax.fori_loop(0, block // TILE, tile, 0)
+        peers(
+            lambda q: remote(
+                term.at[q, sl, :], landed.at[t, sl, :], rs_send.at[b], rs_recv.at[b], z, q
+            ).start()
+        )
+
+    def finish(b):
+        sl = at_block(b)
+        drain(landed.at[pl.ds(0, NT - 1), sl, :], rs_recv.at[b])
+        landed[t, sl, :] = term[t, sl, :]
+        total = landed[0, sl, :].astype(F32)
+        for j in range(1, NT):
+            total = total + landed[j, sl, :].astype(F32)
+        fin[sl, :] = total.astype(BF16)
+
+        @pl.when(away)
+        def _():
+            remote(
+                fin.at[sl, :], fin_land.at[sl, :], fin_send.at[b], fin_recv.at[b], pz, pt
+            ).start()
+
+    def features():
+        for k in range(2):
+            pg = jnp.dot(dval[z, k], proj_out[k], preferred_element_type=F32)
+            pin_k = jnp.concatenate([pin_all[q, k] for q in range(NT)], axis=0)
+            prod = jnp.dot(pin_k, pg, preferred_element_type=F32, precision=lax.Precision.HIGHEST)
+            prod = jnp.concatenate([prod, jnp.zeros_like(prod)], axis=1)
+            for q in range(NT):
+                feat_send[q, k] = prod[q * (rank // NT) : (q + 1) * (rank // NT)]
+        peers(lambda q: remote(feat_send.at[q], feat_recv.at[t], ft_send, ft_recv, z, q).start())
+
+    own = pl.ds(pl.multiple_of(z * block, block), block)
+    forward(z, lambda: tokens[:, own])
+
+    drain(pin_recv.at[pl.ds(0, NT - 1)], ps_recv)
+    pin_recv[t] = pin_send[t]
+    total = pin_recv[0]
+    for j in range(1, NT):
+        total = total + pin_recv[j]
+    pin_all[t] = total
+    peers(lambda q: remote(pin_all.at[t], pin_all.at[t], pa_send, pa_recv, z, q).start())
+
+    for k in range(3):
+        p = dests[k]
+        drain(tok.at[p, pl.ds(0, rows - share), :], a2_recv.at[p])
+        forward(p, lambda: tok[p])
+        reduce(k, 0)
+    drain(pin_all.at[pl.ds(0, NT - 1)], pa_recv)
+
+    def step(s, carry):
+        @pl.when(s + 1 < rounds)
+        def _():
+            for k in range(3):
+                reduce(k, s + 1)
+
+        @pl.when(s < rounds)
+        def _():
+            root(s)
+
+        @pl.when(s >= 1)
+        def _():
+            onward(s - 1)
+
+        @pl.when(s == rounds - 1)
+        def _():
+            features()
+
+        @pl.when(jnp.logical_and(s >= 2, s % 2 == 0))
+        def _():
+            backward(s // 2 - 1)
+
+        @pl.when(jnp.logical_and(s >= 4, s % 2 == 0))
+        def _():
+            finish(s // 2 - 2)
+
+        return carry
+
+    lax.fori_loop(0, rounds + 1, step, 0)
+    blocks = rounds // 2
+    finish(blocks - 1)
+
+    drain(feat_recv.at[pl.ds(0, NT - 1)], ft_recv)
+    feat_recv[t] = feat_send[t]
+    total = feat_recv[0]
+    for j in range(1, NT):
+        total = total + feat_recv[j]
+    feat_out[0] = total[:, :, :rank]
+
+    @pl.when(away)
+    def _():
+        def land(b, c):
+            drain(fin_land.at[at_block(b), :], fin_recv.at[b])
+            drain(fin.at[at_block(b), :], fin_send.at[b])
+            return c
+
+        lax.fori_loop(0, blocks, land, 0)
+        grad_out[...] = fin_land[...]
+
+    @pl.when(jnp.logical_not(away))
+    def _():
+        grad_out[...] = fin[...]
+
+    for d in range(NDP - 1):
+        drain(tok.at[0, my_rows, :], a1_send.at[d])
+    for p in dests:
+        drain(tok.at[0, pl.ds(0, rows - share), :], a2_send.at[p])
+    drain(pin_send.at[pl.ds(0, NT - 1)], ps_send)
+    drain(pin_all.at[pl.ds(0, NT - 1)], pa_send)
+    drain(feat_send.at[pl.ds(0, NT - 1)], ft_send)
+
+    def left(r, c):
+        sl = at_round(r)
+        for k in range(3):
+            drain(part.at[k, :, sl, :], red_send.at[k, r])
+
+            @pl.when(mid)
+            def _():
+                drain(part.at[k, :, sl, :], fwd_send.at[k, r])
+
+        @pl.when(z < NDP - 1)
+        def _():
+            drain(part.at[0, :, sl, :], root_send.at[0, r])
+
+        @pl.when(z > 0)
+        def _():
+            drain(part.at[0, :, sl, :], root_send.at[1, r])
+
+        return c
+
+    lax.fori_loop(0, rounds, left, 0)
+
+    def left_rs(b, c):
+        drain(term.at[pl.ds(0, NT - 1), at_block(b), :], rs_send.at[b])
+        return c
+
+    lax.fori_loop(0, blocks, left_rs, 0)
+
+
+def fused_call(tokens, hidden_grad, gate_weight, up_weight, proj_in, proj_out):
+    rows, width = tokens.shape
+    block, hid = gate_weight.shape
+    rank = proj_in.shape[2]
+    band = width // NT
+    rounds = rows // ROUND
+    dma = pltpu.SemaphoreType.DMA
+    vmem = pl.BlockSpec(memory_space=pltpu.VMEM)
+    hbm = pl.BlockSpec(memory_space=pl.ANY)
+    small = pltpu.VMEM((NT, 2, rank // NT, 128), F32)
+    wide = (2, rows, hid)
+    return pl.pallas_call(
+        fused,
+        out_shape=(
+            jax.ShapeDtypeStruct((rows, band), BF16),
+            jax.ShapeDtypeStruct((1, 2, rank // NT, rank), F32),
+        ),
+        in_specs=[vmem, vmem, hbm, hbm, vmem, vmem],
+        out_specs=(vmem, vmem),
+        scratch_shapes=[
+            pltpu.VMEM((block, hid), BF16),
+            pltpu.VMEM((block, hid), BF16),
+            pltpu.VMEM((NDP, rows, block), BF16),
+            pltpu.VMEM((NDP,) + wide, F32),
+            pltpu.VMEM((3,) + wide, BF16),
+            pltpu.VMEM((5,) + wide, BF16),
+            pltpu.VMEM((NDP,) + wide, BF16),
+            pltpu.VMEM((NT, rows, band), BF16),
+            pltpu.VMEM((NT, rows, band), BF16),
+            pltpu.VMEM((rows, band), BF16),
+            pltpu.VMEM((rows, band), BF16),
+            small, small, small, small, small,
+            dma((2,)), dma((3,)), dma((NDP,)), dma((NDP,)), dma((NDP,)),
+            dma((3, rounds)), dma((5, rounds)), dma((2, rounds)), dma((3, rounds)),
+            dma((NDP, rounds)), dma((rounds // 2,)), dma((rounds // 2,)),
+            dma((rounds // 2,)), dma((rounds // 2,)),
+            dma(()), dma(()), dma(()), dma(()), dma(()), dma(()),
+        ],
+        compiler_params=pltpu.CompilerParams(
+            collective_id=0, has_side_effects=True, vmem_limit_bytes=60 * 2**20
+        ),
+        cost_estimate=pl.CostEstimate(
+            flops=16 * rows * NDP * block * hid // 2, bytes_accessed=8 * block * hid, transcendentals=rows * hid
+        ),
+    )(tokens, hidden_grad, gate_weight, up_weight, proj_in, proj_out)
+
+
+def fits(mesh, tokens, gate_weight, proj_in):
+    n_dp, n_tensor = mesh.shape["dp"], mesh.shape["tensor"]
+    rows, width = tokens.shape[0] // n_dp, tokens.shape[1]
+    hid = gate_weight.shape[1] // n_tensor
+    return (
+        (n_dp, n_tensor) == (NDP, NT)
+        and rows == SEQ_LEN
+        and width % (NT * TILE) == 0
+        and hid % TILE == 0
+        and proj_in.shape[2] == 64
+    )
+
+
 def solution(mesh):
     placed = (
         P("dp", None),
@@ -72,13 +466,17 @@
         P(None, "tensor", None),
     )
 
-    def body(*args):
-        return shards(mesh.shape["dp"], mesh.shape["tensor"], *args)
-
-    return jax.shard_map(
-        body,
-        mesh=mesh,
-        in_specs=placed,
-        out_specs=(P("dp", "tensor"), P("dp", None, "tensor", None)),
-        check_vma=False,
-    )
+    def program(*args):
+        if fits(mesh, args[0], args[2], args[4]):
+            body = fused_call
+        else:
+            body = functools.partial(shards, mesh.shape["dp"], mesh.shape["tensor"])
+        return jax.shard_map(
+            body,
+            mesh=mesh,
+            in_specs=placed,
+            out_specs=(P("dp", "tensor"), P("dp", None, "tensor", None)),
+            check_vma=False,
+        )(*args)
+
+    return program

time: 388 us -> 222 us (0.57)
  waiting for transfers between devices: 294 us -> 0 us
  Pallas kernels: 0 us -> 213 us
  matrix products: 41 us -> 0 us
  between operations: 14.2 us -> 0.64 us
  blocking collectives: 11.3 us -> 0 us
  local copies, waits for them, and re-layouts: 15.7 us -> 7.2 us
  starting transfers between devices: 6.35 us -> 0 us
    pallas_call x0 -> x1, Pallas kernels: none -> 213 us  [fused_call(): pl.pallas_call(fused, out_shape=(jax.ShapeDtypeStruct((rows, band), BF16)...]
    reduce_scatter x4 -> x0, waiting for transfers between devices: 142 us -> none  [the longest x1 40.9 us: shards(): lax.psum_scatter(gate_part, 'dp', scatter_dimension=0, tiled=True)]
    all_gather x3 -> x0, waiting for transfers between devices: 101 us -> none  [the longest x1 40 us: shards(): d_gate_all = lax.all_gather(d_gate, 'dp', axis=0, tiled=True)]
    psum x1 -> x0, waiting for transfers between devices: 49.9 us -> none  [shards(): projected_in = lax.psum(in_partial, 'tensor')]
    dot_general x7 -> x0, matrix products: 39 us -> none  [the longest x1 10.1 us: shards(): jnp.einsum('tf,df->td', d_up_all, up_weight, preferred_element_type=F32)]
    all_to_all x1 -> x0, blocking collectives: 11.3 us -> none  [shards(): mine = lax.all_to_all(mine, 'dp', 0, 0)]
    ppermute x1 -> x0, starting transfers between devices: 5.84 us -> none  [shards(): input_grad = lax.ppermute(piece, ('dp', 'tensor'), pairs)]
    reshape x2 -> x0, local copies, waits for them, and re-layouts: 4.69 us -> none  [the longest x1 4.5 us: shards(): term.reshape(n_dp, rows, halves, band).transpose(0, 2, 1, 3)]
  transfers between devices with their start and end apart: 9 -> 0, of which waited for: 8 -> 0; matrix products, arithmetic and copies ran while one was open for 6% -> 0% of each run, Pallas kernels for 0% -> 0%
where the time goes in v1:
time: 222 us; the launch traced here: 221 us
  Pallas kernels  213 us (96%)
  local copies, waits for them, and re-layouts  7.2 us (3%)
    pallas_call x1, Pallas kernels, fused_call(): pl.pallas_call(fused, out_shape=(jax.ShapeDtypeStruct((rows, band), BF16)...  213 us
    unnamed x4, local copies, waits for them, and re-layouts  7.2 us

profile of v1, /device:TPU:7, one launch (start us, length us, event | category | flops | bytes accessed | tf_op | source)
XLA Modules:
  0.0 221.2 jit_solution(8348088741416382231)
XLA Ops:
  0.6 2.0 copy.8.proj_in
  2.6 2.3 %copy.9.proj_out = bf16[2,1792,64]{2,1,0:T(8,128)(2,1)} copy(bf16[2,1792,64]{1,2,0:T(8,128)(2,1)} %param.11) | data formatting | bytes 917504 | tf_op args[5]
  4.9 213.3 %shard_map.77 = (bf16[128,1024]{1,0:T(8,128)(2,1)}, f32[1,2,8,64]{3,2,1,0:T(8,128)}) custom-call(bf16[128,8192]{1,0:T(8,128)(2,1)} %tokens.1, bf16[128,1792]{1,0:T(8,128)(2,1)} %hidden.1, bf16[2048,1792]{1,0:T(8,128)(2,1)} %gate_hbm.1, bf16[2048,1792]{1,0:T(8,128)(2,1)} %up_hbm.1, bf16[2,1024,64]{2,1,0:T(8,128)(2,1)} %copy.8.proj_in, ...), custom_call_target="tpu_custom_call" | custom-call | flops 15032385536 | bytes 29360128 | tf_op jit(solution)/shard_map/pallas_call | solution.py:410
  218.2 1.7 copy.12
  219.9 1.3 copy.13

commit v2 on v1

--- a/solution.py
+++ b/solution.py
@@ -76,7 +76,7 @@
     tokens, hidden, gate_hbm, up_hbm, proj_in, proj_out, grad_out, feat_out,
     wg, wu, tok, acc, part, recv, dval, term, landed, fin, fin_land,
     pin_send, pin_recv, pin_all, feat_send, feat_recv,
-    w_sem, a1_send, a1_recv, a2_send, a2_recv, red_send, red_recv,
+    w_sem, a1_send, a1_recv, a2_send, a2_recv, a3_send, a3_recv, red_send, red_recv,
     root_send, fwd_send, bc_recv, rs_send, rs_recv, fin_send, fin_recv,
     ps_send, ps_recv, pa_send, pa_recv, ft_send, ft_recv,
 ):
@@ -160,11 +160,19 @@
 
     for p in dests:
         drain(tok.at[p, my_rows, :], a1_recv.at[p])
-        peers(
-            lambda q: remote(
-                tok.at[p, my_rows, :], tok.at[p, my_rows, :], a2_send.at[p], a2_recv.at[p], z, q
+        for d in range(1, NT // 2):
+            remote(
+                tok.at[p, my_rows, :], tok.at[p, my_rows, :],
+                a2_send.at[p], a2_recv.at[p], z, lax.rem(t + 2 * d, NT),
             ).start()
-        )
+    for p in dests:
+        drain(tok.at[p, pl.ds(0, 3 * share), :], a2_recv.at[p])
+        for d in range(NT // 2):
+            q_rows = pl.ds(pl.multiple_of(lax.rem(t + 2 * d, NT) * share, share), share)
+            remote(
+                tok.at[p, q_rows, :], tok.at[p, q_rows, :],
+                a3_send.at[p], a3_recv.at[p], z, t + 1 - 2 * (t % 2),
+            ).start()
     cg.wait()
     cu.wait()
 
@@ -228,14 +236,13 @@
         def _():
             bcast(z, r, root_send.at[1, r], z - 1)
 
-    def onward(r):
-        for k in (2, 1, 0):
-            p = dests[k]
-            drain(dval.at[p, :, at_round(r), :], bc_recv.at[p, r])
-
-            @pl.when(mid)
-            def _():
-                bcast(p, r, fwd_send.at[k, r], z - ways[k])
+    def onward(k, r):
+        p = dests[k]
+        drain(dval.at[p, :, at_round(r), :], bc_recv.at[p, r])
+
+        @pl.when(mid)
+        def _():
+            bcast(p, r, fwd_send.at[k, r], z - ways[k])
 
     def at_block(b):
         return pl.ds(pl.multiple_of(b * brows, brows), brows)
@@ -302,40 +309,56 @@
 
     for k in range(3):
         p = dests[k]
-        drain(tok.at[p, pl.ds(0, rows - share), :], a2_recv.at[p])
+        drain(tok.at[p, pl.ds(0, rows // 2), :], a3_recv.at[p])
         forward(p, lambda: tok[p])
-        reduce(k, 0)
     drain(pin_all.at[pl.ds(0, NT - 1)], pa_recv)
 
+    def inner(p):
+        return (p % 2) * (1 - p // 2) + (p // 2) * (1 - p % 2)
+
+    ups = (1 - low, 1 - z % 2, 1 - low)
+    hops = tuple(z * u + (NDP - 1 - z) * (1 - u) for u in ups)
+    root_lag = 3 - inner(z)
+    on_lags = tuple(3 - inner(p) + w * (p - z) for p, w in zip(dests, ways))
+    last_lag = 6 - inner(z)
+
+    def within(r):
+        return jnp.logical_and(r >= 0, r < rounds)
+
     def step(s, carry):
-        @pl.when(s + 1 < rounds)
-        def _():
-            for k in range(3):
-                reduce(k, s + 1)
-
-        @pl.when(s < rounds)
-        def _():
-            root(s)
-
-        @pl.when(s >= 1)
-        def _():
-            onward(s - 1)
-
-        @pl.when(s == rounds - 1)
+        for k in range(3):
+
+            @pl.when(within(s - hops[k]))
+            def _():
+                reduce(k, s - hops[k])
+
+        @pl.when(within(s - root_lag))
+        def _():
+            root(s - root_lag)
+
+        for k in (2, 1, 0):
+
+            @pl.when(within(s - on_lags[k]))
+            def _():
+                onward(k, s - on_lags[k])
+
+        @pl.when(s - root_lag == rounds - 1)
         def _():
             features()
 
-        @pl.when(jnp.logical_and(s >= 2, s % 2 == 0))
-        def _():
-            backward(s // 2 - 1)
-
-        @pl.when(jnp.logical_and(s >= 4, s % 2 == 0))
-        def _():
-            finish(s // 2 - 2)
+        done = s - last_lag + 1
+
+        @pl.when(jnp.logical_and(within(done - 1), done % 2 == 0))
+        def _():
+            backward(done // 2 - 1)
+
+            @pl.when(done >= 4)
+            def _():
+                finish(done // 2 - 2)
 
         return carry
 
-    lax.fori_loop(0, rounds + 1, step, 0)
+    lax.fori_loop(0, rounds + 6, step, 0)
     blocks = rounds // 2
     finish(blocks - 1)
 
@@ -363,7 +386,8 @@
     for d in range(NDP - 1):
         drain(tok.at[0, my_rows, :], a1_send.at[d])
     for p in dests:
-        drain(tok.at[0, pl.ds(0, rows - share), :], a2_send.at[p])
+        drain(tok.at[0, pl.ds(0, 3 * share), :], a2_send.at[p])
+        drain(tok.at[0, pl.ds(0, rows // 2), :], a3_send.at[p])
     drain(pin_send.at[pl.ds(0, NT - 1)], ps_send)
     drain(pin_all.at[pl.ds(0, NT - 1)], pa_send)
     drain(feat_send.at[pl.ds(0, NT - 1)], ft_send)
@@ -428,7 +452,7 @@
             pltpu.VMEM((rows, band), BF16),
             pltpu.VMEM((rows, band), BF16),
             small, small, small, small, small,
-            dma((2,)), dma((3,)), dma((NDP,)), dma((NDP,)), dma((NDP,)),
+            dma((2,)), dma((3,)), dma((NDP,)), dma((NDP,)), dma((NDP,)), dma((NDP,)), dma((NDP,)),
             dma((3, rounds)), dma((5, rounds)), dma((2, rounds)), dma((3, rounds)),
             dma((NDP, rounds)), dma((rounds // 2,)), dma((rounds // 2,)),
             dma((rounds // 2,)), dma((rounds // 2,)),

time: 222 us -> 170 us (0.77)
  Pallas kernels: 213 us -> 162 us
    pallas_call x1, Pallas kernels: 213 us -> 162 us  [fused_call(): pl.pallas_call(fused, out_shape=(jax.ShapeDtypeStruct((rows, band), BF16)...]
where the time goes in v2:
time: 170 us
  Pallas kernels  162 us (95%)
  local copies, waits for them, and re-layouts  7.2 us (4%)
    pallas_call x1, Pallas kernels, fused_call(): pl.pallas_call(fused, out_shape=(jax.ShapeDtypeStruct((rows, band), BF16)...  162 us
    unnamed x4, local copies, waits for them, and re-layouts  7.2 us

profile of v2, /device:TPU:7, one launch (start us, length us, event | category | flops | bytes accessed | tf_op | source)
XLA Modules:
  0.0 170.2 jit_solution(1081163687587864927)
XLA Ops:
  0.6 2.0 %copy.8.proj_in = bf16[2,1024,64]{2,1,0:T(8,128)(2,1)} copy(bf16[2,1024,64]{1,2,0:T(8,128)(2,1)} %param.10) | data formatting | bytes 524288 | tf_op args[4]
  2.6 2.3 %copy.9.proj_out = bf16[2,1792,64]{2,1,0:T(8,128)(2,1)} copy(bf16[2,1792,64]{1,2,0:T(8,128)(2,1)} %param.11) | data formatting | bytes 917504 | tf_op args[5]
  4.9 162.3 %shard_map.77 = (bf16[128,1024]{1,0:T(8,128)(2,1)}, f32[1,2,8,64]{3,2,1,0:T(8,128)}) custom-call(bf16[128,8192]{1,0:T(8,128)(2,1)} %tokens.1, bf16[128,1792]{1,0:T(8,128)(2,1)} %hidden.1, bf16[2048,1792]{1,0:T(8,128)(2,1)} %gate_hbm.1, bf16[2048,1792]{1,0:T(8,128)(2,1)} %up_hbm.1, bf16[2,1024,64]{2,1,0:T(8,128)(2,1)} %copy.8.proj_in, ...), custom_call_target="tpu_custom_call" | custom-call | flops 15032385536 | bytes 29360128 | tf_op jit(solution)/shard_map/pallas_call | solution.py:434
  167.2 1.7 copy.12
  168.9 1.3 copy.13

commit v3 on v2

--- a/solution.py
+++ b/solution.py
@@ -311,6 +311,11 @@
         p = dests[k]
         drain(tok.at[p, pl.ds(0, rows // 2), :], a3_recv.at[p])
         forward(p, lambda: tok[p])
+
+        @pl.when(edge)
+        def _():
+            reduce(k, 0)
+
     drain(pin_all.at[pl.ds(0, NT - 1)], pa_recv)
 
     def inner(p):
@@ -328,7 +333,7 @@
     def step(s, carry):
         for k in range(3):
 
-            @pl.when(within(s - hops[k]))
+            @pl.when(jnp.logical_and(within(s - hops[k]), jnp.logical_or(mid, s > 0)))
             def _():
                 reduce(k, s - hops[k])
 

time: 170 us -> 166 us (0.976)
  Pallas kernels: 162 us -> 158 us
    pallas_call x1, Pallas kernels: 162 us -> 158 us  [fused_call(): pl.pallas_call(fused, out_shape=(jax.ShapeDtypeStruct((rows, band), BF16)...]
where the time goes in v3:
time: 166 us
  Pallas kernels  158 us (95%)
  local copies, waits for them, and re-layouts  7.2 us (4%)
    pallas_call x1, Pallas kernels, fused_call(): pl.pallas_call(fused, out_shape=(jax.ShapeDtypeStruct((rows, band), BF16)...  158 us
    unnamed x4, local copies, waits for them, and re-layouts  7.2 us

profile of v3, /device:TPU:7, one launch (start us, length us, event | category | flops | bytes accessed | tf_op | source)
XLA Modules:
  0.0 165.5 jit_solution(7268124038126125272)
XLA Ops:
  0.6 2.0 %copy.8.proj_in = bf16[2,1024,64]{2,1,0:T(8,128)(2,1)} copy(bf16[2,1024,64]{1,2,0:T(8,128)(2,1)} %param.10) | data formatting | bytes 524288 | tf_op args[4]
  2.6 2.3 %copy.9.proj_out = bf16[2,1792,64]{2,1,0:T(8,128)(2,1)} copy(bf16[2,1792,64]{1,2,0:T(8,128)(2,1)} %param.11) | data formatting | bytes 917504 | tf_op args[5]
  4.9 157.7 %shard_map.77 = (bf16[128,1024]{1,0:T(8,128)(2,1)}, f32[1,2,8,64]{3,2,1,0:T(8,128)}) custom-call(bf16[128,8192]{1,0:T(8,128)(2,1)} %tokens.1, bf16[128,1792]{1,0:T(8,128)(2,1)} %hidden.1, bf16[2048,1792]{1,0:T(8,128)(2,1)} %gate_hbm.1, bf16[2048,1792]{1,0:T(8,128)(2,1)} %up_hbm.1, bf16[2,1024,64]{2,1,0:T(8,128)(2,1)} %copy.8.proj_in, ...), custom_call_target="tpu_custom_call" | custom-call | flops 15032385536 | bytes 29360128 | tf_op jit(solution)/shard_map/pallas_call | solution.py:439
  162.6 1.7 %copy.12 = bf16[128,1024]{1,0:T(8,128)(2,1)} copy(bf16[128,1024]{1,0:T(8,128)(2,1)} %get-tuple-element.4) | data formatting | bytes 524288
  164.2 1.3 copy.13
